TPU v7x, 32 devices: a whole 2x2x4 slice. The times are simulated.
32 devices in a mesh: rep: 16 (over z, y, x), sp: 2 (over core).
Axes of the slice: x: 2, y: 2, z: 4, core: 2. Of those that a mesh axis runs over, the one named last changes fastest.
Arguments:
- level_four: bfloat16 [16, 96, 96, 256], P('rep', 'sp'), may hold values from -25 to 25
- level_six: bfloat16 [16, 24, 24, 256], P('rep', 'sp'), may hold values from -25 to 25
- conv_weight: bfloat16 [9, 256, 256], replicated, may hold values from -0.125 to 0.125
- bn_gain: float32 [2, 256], replicated, may hold values from 0.1 to 1.9
- bn_shift: float32 [2, 256], replicated, may hold values from -3 to 3
- cotan_four: bfloat16 [16, 96, 96, 256], P('rep', 'sp'), may hold values from -6 to 6
- cotan_six: bfloat16 [16, 24, 24, 256], P('rep', 'sp'), may hold values from -6 to 6
Outputs:
- grad_four: bfloat16 [16, 96, 96, 256], P('rep', 'sp')
- grad_six: bfloat16 [16, 24, 24, 256], P('rep', 'sp')
- grad_weight: float32 [9, 256, 256], P(None, 'sp')
- grad_gain: float32 [2, 256], replicated
- grad_shift: float32 [2, 256], replicated
All inputs are finite; a program needn't handle non-finite values.
Results may differ from a plain program's by a relative error of at most 0.0052.
Values may be sent and summed in bfloat16 or wider, within the bound.
No kernel may reach another device: no remote copies, remote signals or barrier semaphores. Data moves between devices by JAX's collectives and lax.ppermute only.
A program may use at most 128 MiB of HBM per device.

v0:
```python
import jax
import jax.numpy as jnp
from jax import lax
from jax.sharding import PartitionSpec as P

GROUP = 16


EPSILON = 1e-05


def padded_2(cells, sides, width):
    for axis, dim in sides:
        count = lax.axis_size(axis)
        ends = count - 1
        head = lax.slice_in_dim(cells, 0, width, axis=dim)
        tail = lax.slice_in_dim(cells, cells.shape[dim] - width, cells.shape[dim], axis=dim)
        cells = jnp.concatenate(
            [
                lax.ppermute(tail, axis, [(i, (i + 1) % count) for i in range(ends)]),
                cells,
                lax.ppermute(head, axis, [((i + 1) % count, i) for i in range(ends)]),
            ],
            axis=dim,
        )
    return cells


def taps_forward(framed, conv_weight, rows, cols):
    padded = jnp.pad(framed, ((0, 0), (0, 0), (1, 1), (0, 0)))
    result = None
    for row_tap in range(3):
        for col_tap in range(3):
            term = jnp.einsum(
                "nhwc,cd->nhwd",
                padded[:, row_tap : row_tap + rows, col_tap : col_tap + cols],
                conv_weight[3 * row_tap + col_tap],
                preferred_element_type=jnp.float32,
            )
            result = term if result is None else result + term
    return result


def taps_backward(framed, conv_weight, rows, cols):
    padded = jnp.pad(framed, ((0, 0), (0, 0), (1, 1), (0, 0)))
    result = None
    for row_tap in range(3):
        for col_tap in range(3):
            term = jnp.einsum(
                "nhwd,cd->nhwc",
                padded[:, 2 - row_tap : 2 - row_tap + rows, 2 - col_tap : 2 - col_tap + cols],
                conv_weight[3 * row_tap + col_tap],
                preferred_element_type=jnp.float32,
            )
            result = term if result is None else result + term
    return result


def taps_weight(framed, gradient, rows, cols):
    padded = jnp.pad(framed, ((0, 0), (0, 0), (1, 1), (0, 0)))
    terms = []
    for row_tap in range(3):
        for col_tap in range(3):
            terms.append(
                jnp.einsum(
                    "nhwc,nhwd->cd",
                    padded[:, row_tap : row_tap + rows, col_tap : col_tap + cols],
                    gradient,
                    preferred_element_type=jnp.float32,
                )
            )
    return jnp.stack(terms)


def group_sum(moments):
    per_tile = lax.psum(moments, "sp")
    everyone = lax.all_gather(per_tile[None], "rep", axis=0, tiled=True)
    first_row = lax.axis_index("rep") // GROUP * GROUP
    group_total = jnp.sum(lax.dynamic_slice_in_dim(everyone, first_row, GROUP, 0), 0)
    all_total = jnp.sum(everyone, 0)
    return (group_total, all_total)


def scale_level(conv, first, second, count):
    mean = first / count
    spread = second / count - mean * mean
    rstd = lax.rsqrt(spread + EPSILON)
    return ((conv - mean) * rstd, rstd)


def slope_level(scaled, cotan, gain, shift):
    normed = scaled * gain + shift
    sigm = jax.nn.sigmoid(normed)
    return cotan.astype(jnp.float32) * sigm * (1.0 + normed * (1.0 - sigm))


def local(level_four, level_six, conv_weight, bn_gain, bn_shift, cotan_four, cotan_six):
    sp_count = lax.axis_size("sp")
    images = level_four.shape[0]
    rows_four, cols_four = (level_four.shape[1], level_four.shape[2])
    rows_six, cols_six = (level_six.shape[1], level_six.shape[2])
    framed_four = padded_2(level_four, (("sp", 1),), 1)
    framed_six = padded_2(level_six, (("sp", 1),), 1)
    conv_four = lax.optimization_barrier(
        taps_forward(framed_four, conv_weight, rows_four, cols_four).astype(jnp.bfloat16)
    ).astype(jnp.float32)
    conv_six = lax.optimization_barrier(
        taps_forward(framed_six, conv_weight, rows_six, cols_six).astype(jnp.bfloat16)
    ).astype(jnp.float32)
    count_four = float(images * GROUP * rows_four * sp_count * cols_four)
    count_six = float(images * GROUP * rows_six * sp_count * cols_six)
    moments = jnp.stack(
        [
            jnp.sum(conv_four, (0, 1, 2)),
            jnp.sum(conv_four * conv_four, (0, 1, 2)),
            jnp.sum(conv_six, (0, 1, 2)),
            jnp.sum(conv_six * conv_six, (0, 1, 2)),
        ]
    )
    group_moments, unused = group_sum(moments)
    scaled_four, rstd_four = scale_level(conv_four, group_moments[0], group_moments[1], count_four)
    scaled_six, rstd_six = scale_level(conv_six, group_moments[2], group_moments[3], count_six)
    slope_four = slope_level(scaled_four, cotan_four, bn_gain[0], bn_shift[0])
    slope_six = slope_level(scaled_six, cotan_six, bn_gain[1], bn_shift[1])
    slopes = jnp.stack(
        [
            jnp.sum(slope_four, (0, 1, 2)),
            jnp.sum(slope_four * scaled_four, (0, 1, 2)),
            jnp.sum(slope_six, (0, 1, 2)),
            jnp.sum(slope_six * scaled_six, (0, 1, 2)),
        ]
    )
    group_slopes, all_slopes = group_sum(slopes)
    dconv_four = (
        bn_gain[0]
        * rstd_four
        * (slope_four - group_slopes[0] / count_four - scaled_four * group_slopes[1] / count_four)
    ).astype(jnp.bfloat16)
    dconv_six = (
        bn_gain[1]
        * rstd_six
        * (slope_six - group_slopes[2] / count_six - scaled_six * group_slopes[3] / count_six)
    ).astype(jnp.bfloat16)
    dframed_four = padded_2(dconv_four, (("sp", 1),), 1)
    dframed_six = padded_2(dconv_six, (("sp", 1),), 1)
    grad_four = taps_backward(dframed_four, conv_weight, rows_four, cols_four).astype(jnp.bfloat16)
    grad_six = taps_backward(dframed_six, conv_weight, rows_six, cols_six).astype(jnp.bfloat16)
    weight_terms = taps_weight(framed_four, dconv_four, rows_four, cols_four) + taps_weight(
        framed_six, dconv_six, rows_six, cols_six
    )
    total_sum = lax.psum(weight_terms, ("rep", "sp"))
    col_share = weight_terms.shape[1] // sp_count
    grad_weight = lax.dynamic_slice_in_dim(
        total_sum, lax.axis_index("sp") * col_share, col_share, 1
    )
    grad_gain = jnp.stack([all_slopes[1], all_slopes[3]])
    grad_shift = jnp.stack([all_slopes[0], all_slopes[2]])
    return (grad_four, grad_six, grad_weight, grad_gain, grad_shift)


def solution(mesh):
    placed = (
        P("rep", "sp", None, None),
        P("rep", "sp", None, None),
        P(),
        P(),
        P(),
        P("rep", "sp", None, None),
        P("rep", "sp", None, None),
    )
    return jax.shard_map(
        local,
        mesh=mesh,
        in_specs=placed,
        out_specs=(
            P("rep", "sp", None, None),
            P("rep", "sp", None, None),
            P(None, "sp", None),
            P(),
            P(),
        ),
        check_vma=False,
    )
```

profile of v0, /device:TPU:0, one launch (start us, length us, event | category | flops | bytes accessed | tf_op | source)
XLA Modules:
  0.0 324.9 jit_solution(4645463058098209993)
XLA Ops:
  7.2 0.7 fusion.299
  7.9 2.3 collective-permute-start.2
  10.3 1.3 collective-permute-start.3
  11.6 0.8 fusion.297
  12.4 3.0 collective-permute-start
  15.5 1.3 collective-permute-start.1
  16.8 0.8 fusion.301
  17.5 4.7 %fusion.63 = f32[48,96,256]{2,1,0:T(8,128)} fusion(bf16[1,48,96,256]{3,2,1,0:T(8,128)(2,1)} %param.7, bf16[9,256,256]{2,1,0:T(8,128)(2,1)} %param.9), kind=kOutput, calls=%fused_computation.86 | convolution fusion | flops 603979776 | bytes 7208960 | tf_op jit(solution)/shard_map/nhwc,cd->nhwd/dot_general | solution.py:34
  24.3 0.5 copy-done.2
  24.8 1.2 fusion.23
  26.0 2.9 fusion.69
  29.0 3.0 fusion.68
  32.0 2.9 fusion.67
  34.9 3.0 fusion.66
  37.9 2.9 fusion.65
  40.8 2.9 fusion.75
  43.7 3.0 fusion.72
  46.7 13.1 %fusion.24 = bf16[1,48,96,256]{3,2,1,0:T(8,128)(2,1)S(1)} fusion(f32[48,96,256]{2,1,0:T(8,128)} %fusion.75, f32[48,96,256]{2,1,0:T(8,128)} %fusion.69, f32[48,96,256]{2,1,0:T(8,128)} %fusion.68, f32[48,96,256]{2,1,0:T(8,128)} %fusion.63, f32[48,96,256]{2,1,0:T(8,128)} %fusion.67, f32[48,96,256]{2,1,0:T(8,128)} %fusion.66, f32[48,96,256]{2,1,0:T(8,128)} %fusion.65, ...), kind=kOutput, calls=%fused_computation.33 | convolution fusion | flops 614596608 | bytes 42598400 | tf_op jit(solution)/shard_map/nhwc,cd->nhwd/dot_general | solution.py:34
  59.8 1.4 copy-done.4
  61.2 0.7 convert_reduce_fusion
  61.9 3.3 %psum.21 = f32[1,4,256]{2,1,0:T(4,128)S(1)} all-reduce(f32[1,4,256]{2,1,0:T(4,128)S(1)} %maximum_bitcast_fusion), channel_id=1, replica_groups=mesh['rep'=16,'sp'=2] {'sp'}, use_global_device_ids=true, to_apply=%region_4.5 | all-reduce | flops 1024 | bytes 8192 | tf_op jit(solution)/shard_map/psum | solution.py:76
  65.2 42.1 %all_gather.6 = f32[16,4,256]{2,1,0:T(4,128)S(1)} all-gather(f32[1,4,256]{2,1,0:T(4,128)S(1)} %psum.21), channel_id=1, replica_groups=mesh['rep'=16,'sp'=2] {'rep'}, dimensions={0}, use_global_device_ids=true | all-gather | bytes 69632 | tf_op jit(solution)/shard_map/all_gather | solution.py:77
  107.3 0.6 fusion.278
  107.9 1.8 fusion.293
  109.7 5.9 %fusion.292 = (f32[256]{0:T(256)S(1)}, f32[256]{0:T(256)S(1)}, f32[1,48,96,256]{3,2,1,0:T(8,128)}) fusion(f32[256]{0:T(256)S(1)} %get-tuple-element.36, f32[256]{0:T(256)S(1)} %bitcast.462, bf16[1,48,96,256]{3,2,1,0:T(8,128)(2,1)} %copy-done.4, f32[256]{0:T(256)S(1)} %bitcast.472, f32[256]{0:T(256)S(1)} %bitcast.465, bf16[1,48,96,256]{3,2,1,0:T(8,128)(2,1)} %param.12), kind=kLoop, calls=%fused_computation.318 | loop fusion | flops 20053504 | bytes 9443328 | tf_op jit(solution)/shard_map/reduce_sum | solution.py:127
  115.6 2.5 psum.22
  118.1 36.0 %all_gather.7 = f32[16,4,256]{2,1,0:T(4,128)S(1)} all-gather(f32[1,4,256]{2,1,0:T(4,128)S(1)} %psum.22), channel_id=1, replica_groups=mesh['rep'=16,'sp'=2] {'rep'}, dimensions={0}, use_global_device_ids=true | all-gather | bytes 69632 | tf_op jit(solution)/shard_map/all_gather | solution.py:77
  154.1 0.6 fusion.300
  154.6 4.4 %fusion.18 = bf16[1,48,96,256]{3,2,1,0:T(8,128)(2,1)S(1)} fusion(bf16[1,48,96,256]{3,2,1,0:T(8,128)(2,1)} %copy-done.4, f32[1,48,96,256]{3,2,1,0:T(8,128)} %get-tuple-element.13, f32[256]{0:T(256)S(1)} %bitcast.469, f32[256]{0:T(256)S(1)} %bitcast.471, f32[256]{0:T(256)S(1)} %get-tuple-element.36, f32[256]{0:T(256)S(1)} %bitcast.463, ...), kind=kLoop, calls=%fused_computation.23 | loop fusion | flops 10616832 | bytes 9442304 | tf_op jit(solution)/shard_map/convert_element_type | solution.py:138
  159.1 0.8 fusion.82
  159.9 0.3 copy-done.9
  160.6 4.0 %fusion.60 = f32[48,96,256]{2,1,0:T(8,128)} fusion(bf16[1,48,96,256]{3,2,1,0:T(8,128)(2,1)S(1)} %fusion.18, bf16[9,256,256]{2,1,0:T(8,128)(2,1)} %param.9), kind=kOutput, calls=%fused_computation.83 | convolution fusion | flops 603979776 | bytes 7208960 | tf_op jit(solution)/shard_map/nhwd,cd->nhwc/dot_general | solution.py:49
  164.6 1.3 collective-permute-start.6
  165.9 1.3 collective-permute-start.7
  167.2 1.3 collective-permute-start.5
  168.5 3.0 collective-permute-start.4
  171.6 0.9 fusion.130
  172.5 0.8 fusion.88
  173.3 0.8 fusion.94
  174.2 1.1 fusion.102
  175.3 0.8 fusion.110
  176.1 0.8 fusion.116
  177.0 0.9 fusion.140
  177.9 0.8 fusion.122
  179.3 0.3 fusion.150
  179.6 0.3 fusion.149
  180.1 0.3 fusion.147
  180.4 0.3 fusion.146
  180.7 0.3 fusion.145
  180.9 1.8 add.247
  182.8 0.6 copy-done.15
  183.4 0.6 pad_maximum_fusion.8
  186.0 0.9 fusion.156
  187.0 1.3 select_maximum_fusion
  188.3 3.1 fusion.31
  191.4 2.9 fusion.32
  194.3 3.0 fusion.33
  197.3 3.0 fusion.34
  200.3 3.0 fusion.39
  203.3 3.0 fusion.28
  206.3 3.0 fusion.36
  209.3 14.6 %fusion.25 = bf16[1,48,96,256]{3,2,1,0:T(8,128)(2,1)} fusion(f32[48,96,256]{2,1,0:T(8,128)} %fusion.28, f32[48,96,256]{2,1,0:T(8,128)} %fusion.31, f32[48,96,256]{2,1,0:T(8,128)} %fusion.32, f32[48,96,256]{2,1,0:T(8,128)} %fusion.60, f32[48,96,256]{2,1,0:T(8,128)} %fusion.33, f32[48,96,256]{2,1,0:T(8,128)} %fusion.34, f32[48,96,256]{2,1,0:T(8,128)} %fusion.39, ...), kind=kOutput, calls=%fused_computation.34 | convolution fusion | flops 614596608 | bytes 42598400 | tf_op jit(solution)/shard_map/nhwd,cd->nhwc/dot_general | solution.py:49
  223.9 91.8 %all-reduce.6.cloned.1.call-done = f32[9,256,256]{2,1,0:T(8,128)} async-done(((f32[9,256,256]{2,1,0:T(8,128)}), f32[9,256,256]{2,1,0:T(8,128)}) %all-reduce.6.cloned.1.call-update) | async-done | bytes 2359312 | tf_op jit(solution)/shard_map/psum | solution.py:151
  315.7 2.4 constant_dynamic-slice_fusion
  (84 shorter events, 5.4 us)
Async XLA Ops:
  7.2 308.6 %all-reduce.6.cloned.1.call-start = ((), (), s32[]{:S(2)}) async-start(), calls=%async_computation | async-start | bytes 4718592 | tf_op jit(solution)/shard_map/psum | solution.py:151
  7.9 14.3 %collective-permute-start.2 = (bf16[1,1,24,256]{3,2,1,0:T(8,128)(2,1)S(1)}, bf16[1,1,24,256]{3,2,1,0:T(8,128)(2,1)S(1)}, u32[]{:S(2)}, u32[]{:S(2)}) collective-permute-start(bf16[1,1,24,256]{3,2,1,0:T(8,128)(2,1)S(1)} %get-tuple-element.21), channel_id=1, source_target_pairs={{0,1},{2,3},{4,5},{6,7},{8,9},{10,11},{12,13},{14,15},{16,17},{18,... | collective-permute-start | bytes 36872 | tf_op jit(solution)/shard_map/ppermute | solution.py:20
  10.3 11.9 %collective-permute-start.3 = (bf16[1,1,24,256]{3,2,1,0:T(8,128)(2,1)S(1)}, bf16[1,1,24,256]{3,2,1,0:T(8,128)(2,1)S(1)}, u32[]{:S(2)}, u32[]{:S(2)}) collective-permute-start(bf16[1,1,24,256]{3,2,1,0:T(8,128)(2,1)S(1)} %get-tuple-element.22), channel_id=1, source_target_pairs={{1,0},{3,2},{5,4},{7,6},{9,8},{11,10},{13,12},{15,14},{17,16},{19,... | collective-permute-start | bytes 36872 | tf_op jit(solution)/shard_map/ppermute | solution.py:22
  12.4 11.9 %collective-permute-start = (bf16[1,1,96,256]{3,2,1,0:T(8,128)(2,1)S(1)}, bf16[1,1,96,256]{3,2,1,0:T(8,128)(2,1)S(1)}, u32[]{:S(2)}, u32[]{:S(2)}) collective-permute-start(bf16[1,1,96,256]{3,2,1,0:T(8,128)(2,1)S(1)} %get-tuple-element.17), channel_id=1, source_target_pairs={{0,1},{2,3},{4,5},{6,7},{8,9},{10,11},{12,13},{14,15},{16,17},{18,... | collective-permute-start | bytes 147464 | tf_op jit(solution)/shard_map/ppermute | solution.py:20
  15.5 8.9 %collective-permute-start.1 = (bf16[1,1,96,256]{3,2,1,0:T(8,128)(2,1)S(1)}, bf16[1,1,96,256]{3,2,1,0:T(8,128)(2,1)S(1)}, u32[]{:S(2)}, u32[]{:S(2)}) collective-permute-start(bf16[1,1,96,256]{3,2,1,0:T(8,128)(2,1)S(1)} %get-tuple-element.18), channel_id=1, source_target_pairs={{1,0},{3,2},{5,4},{7,6},{9,8},{11,10},{13,12},{15,14},{17,16},{19,... | collective-permute-start | bytes 147464 | tf_op jit(solution)/shard_map/ppermute | solution.py:22
  17.5 4.7 %copy-start.21 = (f32[2,256]{1,0:T(2,128)S(1)}, f32[2,256]{1,0:T(2,128)}, u32[]{:S(2)}) copy-start(f32[2,256]{1,0:T(2,128)} %param.11) | copy-start | bytes 6148
  17.5 4.7 %copy-start.8 = (bf16[1,12,24,256]{3,2,1,0:T(8,128)(2,1)S(1)}, bf16[1,12,24,256]{3,2,1,0:T(8,128)(2,1)}, u32[]{:S(2)}) copy-start(bf16[1,12,24,256]{3,2,1,0:T(8,128)(2,1)} %param.8) | copy-start | bytes 442372
  17.5 4.8 %copy-start.5 = (bf16[9,256,256]{2,1,0:T(8,128)(2,1)S(1)}, bf16[9,256,256]{2,1,0:T(8,128)(2,1)}, u32[]{:S(2)}) copy-start(bf16[9,256,256]{2,1,0:T(8,128)(2,1)} %param.9) | copy-start | bytes 3538948
  23.2 1.7 copy-start.2
  24.3 1.7 copy-start.6
  59.8 1.4 copy-start.4
  107.3 8.3 %copy-start.10 = (f32[1,256]{1,0:T(1,128)}, f32[1,256]{1,0:T(1,128)S(1)}, u32[]{:S(2)}) copy-start(f32[1,256]{1,0:T(1,128)S(1)} %get-tuple-element.29) | copy-start | bytes 3076
  107.9 7.7 %copy-start.12 = (f32[256]{0:T(256)}, f32[256]{0:T(256)S(1)}, u32[]{:S(2)}) copy-start(f32[256]{0:T(256)S(1)} %get-tuple-element.34) | copy-start | bytes 3076
  154.6 4.4 %copy-start.16 = (f32[1,256]{1,0:T(1,128)}, f32[1,256]{1,0:T(1,128)S(1)}, u32[]{:S(2)}) copy-start(f32[1,256]{1,0:T(1,128)S(1)} %get-tuple-element.28) | copy-start | bytes 3076
  154.6 5.3 %copy-start.14 = (f32[1,256]{1,0:T(1,128)}, f32[1,256]{1,0:T(1,128)S(1)}, u32[]{:S(2)}) copy-start(f32[1,256]{1,0:T(1,128)S(1)} %get-tuple-element.26) | copy-start | bytes 3076
  159.0 18.9 %copy-start = (bf16[1,48,96,256]{3,2,1,0:T(8,128)(2,1)}, bf16[1,48,96,256]{3,2,1,0:T(8,128)(2,1)S(1)}, u32[]{:S(2)}) copy-start(bf16[1,48,96,256]{3,2,1,0:T(8,128)(2,1)S(1)} %fusion.18) | copy-start | bytes 7077892
  159.0 1.2 copy-start.9
  159.1 1.2 copy-start.11
  159.1 1.2 copy-start.13
  159.1 1.2 copy-start.18
  160.6 10.9 %copy-start.3 = (bf16[1,48,96,256]{3,2,1,0:T(8,128)(2,1)S(1)}, bf16[1,48,96,256]{3,2,1,0:T(8,128)(2,1)}, u32[]{:S(2)}) copy-start(bf16[1,48,96,256]{3,2,1,0:T(8,128)(2,1)} %param.7) | copy-start | bytes 7077892
  164.6 19.4 %collective-permute-start.6 = (bf16[1,1,24,256]{3,2,1,0:T(8,128)(2,1)S(1)}, bf16[1,1,24,256]{3,2,1,0:T(8,128)(2,1)S(1)}, u32[]{:S(2)}, u32[]{:S(2)}) collective-permute-start(bf16[1,1,24,256]{3,2,1,0:T(8,128)(2,1)S(1)} %get-tuple-element.19), channel_id=1, source_target_pairs={{0,1},{2,3},{4,5},{6,7},{8,9},{10,11},{12,13},{14,15},{16,17},{18,... | collective-permute-start | bytes 36872 | tf_op jit(solution)/shard_map/ppermute | solution.py:20
  165.9 18.1 %collective-permute-start.7 = (bf16[1,1,24,256]{3,2,1,0:T(8,128)(2,1)S(1)}, bf16[1,1,24,256]{3,2,1,0:T(8,128)(2,1)S(1)}, u32[]{:S(2)}, u32[]{:S(2)}) collective-permute-start(bf16[1,1,24,256]{3,2,1,0:T(8,128)(2,1)S(1)} %get-tuple-element.20), channel_id=1, source_target_pairs={{1,0},{3,2},{5,4},{7,6},{9,8},{11,10},{13,12},{15,14},{17,16},{19,... | collective-permute-start | bytes 36872 | tf_op jit(solution)/shard_map/ppermute | solution.py:22
  167.2 19.7 %collective-permute-start.5 = (bf16[1,1,96,256]{3,2,1,0:T(8,128)(2,1)S(1)}, bf16[1,1,96,256]{3,2,1,0:T(8,128)(2,1)S(1)}, u32[]{:S(2)}, u32[]{:S(2)}) collective-permute-start(bf16[1,1,96,256]{3,2,1,0:T(8,128)(2,1)S(1)} %get-tuple-element.15), channel_id=1, source_target_pairs={{1,0},{3,2},{5,4},{7,6},{9,8},{11,10},{13,12},{15,14},{17,16},{19,... | collective-permute-start | bytes 147464 | tf_op jit(solution)/shard_map/ppermute | solution.py:22
  168.5 18.4 %collective-permute-start.4 = (bf16[1,1,96,256]{3,2,1,0:T(8,128)(2,1)S(1)}, bf16[1,1,96,256]{3,2,1,0:T(8,128)(2,1)S(1)}, u32[]{:S(2)}, u32[]{:S(2)}) collective-permute-start(bf16[1,1,96,256]{3,2,1,0:T(8,128)(2,1)S(1)} %get-tuple-element.16), channel_id=1, source_target_pairs={{0,1},{2,3},{4,5},{6,7},{8,9},{10,11},{12,13},{14,15},{16,17},{18,... | collective-permute-start | bytes 147464 | tf_op jit(solution)/shard_map/ppermute | solution.py:20
  182.7 0.7 copy-start.15
  182.7 0.7 copy-start.17
  182.7 0.7 copy-start.19
  182.7 0.7 copy-start.20
  182.7 1.4 copy-start.7
  185.0 2.0 copy-start.1
Sparse Core Ops, SparseCore 0:
  182.9 132.7 all-reduce.5
where the time goes:
time: 326 us; the launch traced here: 325 us
  matrix products  93 us (29%)
  waiting for transfers between devices  91.9 us (28%)
  blocking collectives  83.8 us (26%)
  other arithmetic  19.1 us (6%)
  starting transfers between devices  14.9 us (5%)
  between operations  14.6 us (4%)
  local copies, waits for them, and re-layouts  7.76 us (2%)
    psum x1, waiting for transfers between devices, local(): total_sum = lax.psum(weight_terms, ('rep', 'sp'))  91.8 us
    all_gather x2, blocking collectives, group_sum(): everyone = lax.all_gather(per_tile[None], 'rep', axis=0, tiled=True)  78 us
    dot_general x18, matrix products, taps_backward(): jnp.einsum('nhwd,cd->nhwc', padded[:, 2 - row_tap:2 - row_tap + rows, 2 -...  42.3 us
    dot_general x18, matrix products, taps_forward(): jnp.einsum('nhwc,cd->nhwd', padded[:, row_tap:row_tap + rows, col_tap:col...  40.3 us
    dot_general x18, matrix products, taps_weight(): jnp.einsum('nhwc,nhwd->cd', padded[:, row_tap:row_tap + rows, col_tap:col...  10.4 us
    ppermute x4, starting transfers between devices, padded_2(): lax.ppermute(tail, axis, [(i, (i + 1) % count) for i in range(ends)])  9.67 us
  transfers between devices with their start and end apart: 9, of which 1 were waited for; matrix products, arithmetic and copies ran while one was open for 18% of the time, Pallas kernels for 0%

commit v1 on v0

--- a/solution.py
+++ b/solution.py
@@ -4,6 +4,7 @@
 from jax.sharding import PartitionSpec as P
 
 GROUP = 16
+RADIX = 4
 
 
 EPSILON = 1e-05
@@ -72,13 +73,67 @@
     return jnp.stack(terms)
 
 
-def group_sum(moments):
-    per_tile = lax.psum(moments, "sp")
-    everyone = lax.all_gather(per_tile[None], "rep", axis=0, tiled=True)
-    first_row = lax.axis_index("rep") // GROUP * GROUP
-    group_total = jnp.sum(lax.dynamic_slice_in_dim(everyone, first_row, GROUP, 0), 0)
-    all_total = jnp.sum(everyone, 0)
-    return (group_total, all_total)
+def digit_groups(count, stride):
+    members = []
+    for base in range(count):
+        if base // stride % RADIX == 0:
+            members.append([base + stride * digit for digit in range(RADIX)])
+    return members
+
+
+def exchange(pieces, stride):
+    groups = digit_groups(lax.axis_size("rep"), stride)
+    return lax.all_to_all(pieces, "rep", 0, 0, axis_index_groups=groups, tiled=True)
+
+
+def moment_sum(moments):
+    count = lax.axis_size("rep")
+    if count == GROUP:
+        total = lax.psum(moments, ("rep", "sp"))
+        return (total, total)
+    groups = [list(range(base, base + GROUP)) for base in range(0, count, GROUP)]
+    total = lax.psum(lax.psum(moments, "sp"), "rep", axis_index_groups=groups)
+    return (total, lax.psum(total, "rep") / GROUP)
+
+
+def slope_sum(slopes):
+    count = lax.axis_size("rep")
+    if count == GROUP:
+        copies = jnp.broadcast_to(slopes[None], (count * lax.axis_size("sp"),) + slopes.shape)
+        total = jnp.sum(lax.all_to_all(copies, ("rep", "sp"), 0, 0, tiled=True), 0)
+        return (total, total)
+    return moment_sum(slopes)
+
+
+def weight_sum(terms):
+    count, sp_count = (lax.axis_size("rep"), lax.axis_size("sp"))
+    share = terms.shape[1] // sp_count
+    own = lax.axis_index("sp")
+    total = lax.dynamic_slice_in_dim(terms, own * share, share, 1)
+    for step in range(1, sp_count):
+        sent = lax.dynamic_slice_in_dim(terms, (own ^ step) * share, share, 1)
+        total = total + lax.ppermute(
+            sent.astype(jnp.bfloat16), "sp", [(i, i ^ step) for i in range(sp_count)]
+        ).astype(jnp.float32)
+    shape = total.shape
+    strides = []
+    stride = 1
+    while stride < count:
+        strides.append(stride)
+        stride = stride * RADIX
+    total = total.reshape(-1, shape[-1])
+    halved = strides[:2]
+    for stride in halved:
+        pieces = total.reshape(RADIX, -1, shape[-1]).astype(jnp.bfloat16)
+        total = jnp.sum(exchange(pieces, stride).astype(jnp.float32), 0)
+    for stride in strides[2:]:
+        pieces = jnp.broadcast_to(total.astype(jnp.bfloat16)[None], (RADIX,) + total.shape)
+        total = jnp.sum(exchange(pieces, stride).astype(jnp.float32), 0)
+    total = total.astype(jnp.bfloat16)
+    for stride in halved[::-1]:
+        pieces = jnp.broadcast_to(total[None], (RADIX,) + total.shape)
+        total = exchange(pieces, stride).reshape(-1, shape[-1])
+    return total.reshape(shape).astype(jnp.float32)
 
 
 def scale_level(conv, first, second, count):
@@ -117,7 +172,7 @@
             jnp.sum(conv_six * conv_six, (0, 1, 2)),
         ]
     )
-    group_moments, unused = group_sum(moments)
+    group_moments, unused = moment_sum(moments)
     scaled_four, rstd_four = scale_level(conv_four, group_moments[0], group_moments[1], count_four)
     scaled_six, rstd_six = scale_level(conv_six, group_moments[2], group_moments[3], count_six)
     slope_four = slope_level(scaled_four, cotan_four, bn_gain[0], bn_shift[0])
@@ -130,7 +185,7 @@
             jnp.sum(slope_six * scaled_six, (0, 1, 2)),
         ]
     )
-    group_slopes, all_slopes = group_sum(slopes)
+    group_slopes, all_slopes = slope_sum(slopes)
     dconv_four = (
         bn_gain[0]
         * rstd_four
@@ -148,11 +203,7 @@
     weight_terms = taps_weight(framed_four, dconv_four, rows_four, cols_four) + taps_weight(
         framed_six, dconv_six, rows_six, cols_six
     )
-    total_sum = lax.psum(weight_terms, ("rep", "sp"))
-    col_share = weight_terms.shape[1] // sp_count
-    grad_weight = lax.dynamic_slice_in_dim(
-        total_sum, lax.axis_index("sp") * col_share, col_share, 1
-    )
+    grad_weight = weight_sum(weight_terms)
     grad_gain = jnp.stack([all_slopes[1], all_slopes[3]])
     grad_shift = jnp.stack([all_slopes[0], all_slopes[2]])
     return (grad_four, grad_six, grad_weight, grad_gain, grad_shift)

time: 326 us -> 218 us (0.67)
  waiting for transfers between devices: 91.9 us -> 13.1 us
  blocking collectives: 83.8 us -> 41.4 us
  starting transfers between devices: 14.9 us -> 34.6 us
  between operations: 14.6 us -> 1.28 us
  matrix products: 93 us -> 96.7 us
    psum x1 -> x0, waiting for transfers between devices: 91.8 us -> none  [local(): total_sum = lax.psum(weight_terms, ('rep', 'sp'))]
    all_gather x2 -> x0, blocking collectives: 78 us -> none  [group_sum(): everyone = lax.all_gather(per_tile[None], 'rep', axis=0, tiled=True)]
    psum x2 -> x1, blocking collectives: 5.75 us -> 41.4 us  [moment_sum(): total = lax.psum(moments, ('rep', 'sp'))]
    all_to_all x0 -> x5, starting transfers between devices: none -> 18.8 us  [the longest x4 13.7 us: exchange(): lax.all_to_all(pieces, 'rep', 0, 0, axis_index_groups=groups, tiled=True)]
    all_to_all x0 -> x5, waiting for transfers between devices: none -> 13.1 us  [the longest x1 8.19 us: slope_sum(): total = jnp.sum(lax.all_to_all(copies, ('rep', 'sp'), 0, 0, tiled=True), 0)]
    dot_general x18, matrix products: 42.3 us -> 46.3 us  [taps_backward(): jnp.einsum('nhwd,cd->nhwc', padded[:, 2 - row_tap:2 - row_tap + rows, 2 -...]
  transfers between devices with their start and end apart: 9 -> 14, of which waited for: 1 -> 4; matrix products, arithmetic and copies ran while one was open for 18% -> 30% of each run, Pallas kernels for 0% -> 0%
where the time goes in v1:
time: 218 us; the launch traced here: 217 us
  matrix products  96.7 us (44%)
  blocking collectives  41.4 us (19%)
  starting transfers between devices  34.6 us (16%)
  other arithmetic  21.8 us (10%)
  waiting for transfers between devices  13.1 us (6%)
  local copies, waits for them, and re-layouts  8.16 us (4%)
    dot_general x18, matrix products, taps_backward(): jnp.einsum('nhwd,cd->nhwc', padded[:, 2 - row_tap:2 - row_tap + rows, 2 -...  46.3 us
    psum x1, blocking collectives, moment_sum(): total = lax.psum(moments, ('rep', 'sp'))  41.4 us
    dot_general x18, matrix products, taps_forward(): jnp.einsum('nhwc,cd->nhwd', padded[:, row_tap:row_tap + rows, col_tap:col...  40.2 us
    all_to_all x4, starting transfers between devices, exchange(): lax.all_to_all(pieces, 'rep', 0, 0, axis_index_groups=groups, tiled=True)  13.7 us
    ppermute x4, starting transfers between devices, padded_2(): lax.ppermute(tail, axis, [(i, (i + 1) % count) for i in range(ends)])  10.5 us
    dot_general x18, matrix products, taps_weight(): jnp.einsum('nhwc,nhwd->cd', padded[:, row_tap:row_tap + rows, col_tap:col...  10.2 us
    all_to_all x1, waiting for transfers between devices, slope_sum(): total = jnp.sum(lax.all_to_all(copies, ('rep', 'sp'), 0, 0, tiled=True), 0)  8.19 us
    reduce_sum x1, other arithmetic, local(): jnp.sum(slope_four, (0, 1, 2))  5.91 us
  transfers between devices with their start and end apart: 14, of which 4 were waited for; matrix products, arithmetic and copies ran while one was open for 30% of the time, Pallas kernels for 0%

profile of v1, /device:TPU:0, one launch (start us, length us, event | category | flops | bytes accessed | tf_op | source)
XLA Modules:
  0.0 217.0 jit_solution(8117455123249914665)
XLA Ops:
  0.6 0.7 fusion.299
  1.4 2.3 %collective-permute-start.2 = (bf16[1,1,24,256]{3,2,1,0:T(8,128)(2,1)S(1)}, bf16[1,1,24,256]{3,2,1,0:T(8,128)(2,1)S(1)}, u32[]{:S(2)}, u32[]{:S(2)}) collective-permute-start(bf16[1,1,24,256]{3,2,1,0:T(8,128)(2,1)S(1)} %get-tuple-element.21), channel_id=1, source_target_pairs={{0,1},{2,3},{4,5},{6,7},{8,9},{10,11},{12,13},{14,15},{16,17},{18,... | collective-permute-start | bytes 36872 | tf_op jit(solution)/shard_map/ppermute | solution.py:21
  3.7 1.3 collective-permute-start.3
  5.0 0.8 fusion.297
  5.8 3.0 %collective-permute-start = (bf16[1,1,96,256]{3,2,1,0:T(8,128)(2,1)S(1)}, bf16[1,1,96,256]{3,2,1,0:T(8,128)(2,1)S(1)}, u32[]{:S(2)}, u32[]{:S(2)}) collective-permute-start(bf16[1,1,96,256]{3,2,1,0:T(8,128)(2,1)S(1)} %get-tuple-element.17), channel_id=1, source_target_pairs={{0,1},{2,3},{4,5},{6,7},{8,9},{10,11},{12,13},{14,15},{16,17},{18,... | collective-permute-start | bytes 147464 | tf_op jit(solution)/shard_map/ppermute | solution.py:21
  8.9 1.3 collective-permute-start.1
  10.2 1.3 fusion.301
  11.5 4.7 %fusion.63 = f32[48,96,256]{2,1,0:T(8,128)} fusion(bf16[1,48,96,256]{3,2,1,0:T(8,128)(2,1)} %param.7, bf16[9,256,256]{2,1,0:T(8,128)(2,1)} %param.9), kind=kOutput, calls=%fused_computation.86 | convolution fusion | flops 603979776 | bytes 7208960 | tf_op jit(solution)/shard_map/nhwc,cd->nhwd/dot_general | solution.py:35
  19.4 1.2 fusion.23
  20.6 3.0 %fusion.69 = f32[48,96,256]{2,1,0:T(8,128)} fusion(bf16[1,50,98,256]{3,2,1,0:T(8,128)(2,1)S(1)} %fusion.23, bf16[9,256,256]{2,1,0:T(8,128)(2,1)S(1)} %copy-done.4), kind=kOutput, calls=%fused_computation.92 | convolution fusion | flops 603979776 | bytes 7208960 | tf_op jit(solution)/shard_map/nhwc,cd->nhwd/dot_general | solution.py:35
  23.6 2.9 %fusion.68 = f32[48,96,256]{2,1,0:T(8,128)} fusion(bf16[1,50,98,256]{3,2,1,0:T(8,128)(2,1)S(1)} %fusion.23, bf16[9,256,256]{2,1,0:T(8,128)(2,1)S(1)} %copy-done.4), kind=kOutput, calls=%fused_computation.91 | convolution fusion | flops 603979776 | bytes 7208960 | tf_op jit(solution)/shard_map/nhwc,cd->nhwd/dot_general | solution.py:35
  26.5 3.0 %fusion.67 = f32[48,96,256]{2,1,0:T(8,128)} fusion(bf16[1,50,98,256]{3,2,1,0:T(8,128)(2,1)S(1)} %fusion.23, bf16[9,256,256]{2,1,0:T(8,128)(2,1)S(1)} %copy-done.4), kind=kOutput, calls=%fused_computation.90 | convolution fusion | flops 603979776 | bytes 7208960 | tf_op jit(solution)/shard_map/nhwc,cd->nhwd/dot_general | solution.py:35
  29.5 3.0 %fusion.66 = f32[48,96,256]{2,1,0:T(8,128)} fusion(bf16[1,50,98,256]{3,2,1,0:T(8,128)(2,1)S(1)} %fusion.23, bf16[9,256,256]{2,1,0:T(8,128)(2,1)S(1)} %copy-done.4), kind=kOutput, calls=%fused_computation.89 | convolution fusion | flops 603979776 | bytes 7208960 | tf_op jit(solution)/shard_map/nhwc,cd->nhwd/dot_general | solution.py:35
  32.5 2.9 %fusion.65 = f32[48,96,256]{2,1,0:T(8,128)} fusion(bf16[1,50,98,256]{3,2,1,0:T(8,128)(2,1)S(1)} %fusion.23, bf16[9,256,256]{2,1,0:T(8,128)(2,1)S(1)} %copy-done.4), kind=kOutput, calls=%fused_computation.88 | convolution fusion | flops 603979776 | bytes 7208960 | tf_op jit(solution)/shard_map/nhwc,cd->nhwd/dot_general | solution.py:35
  35.4 2.9 %fusion.75 = f32[48,96,256]{2,1,0:T(8,128)} fusion(bf16[1,1,96,256]{3,2,1,0:T(8,128)(2,1)S(1)} %collective-permute-done.1, bf16[1,48,96,256]{3,2,1,0:T(8,128)(2,1)S(1)} %copy-done.1, bf16[9,256,256]{2,1,0:T(8,128)(2,1)S(1)} %copy-done.4), kind=kOutput, calls=%fused_computation.95 | convolution fusion | flops 605159424 | bytes 7258112 | tf_op jit(solution)/shard_map/nhwc,cd->nhwd/dot_general | solution.py:35
  38.4 3.0 %fusion.72 = f32[48,96,256]{2,1,0:T(8,128)} fusion(bf16[1,48,96,256]{3,2,1,0:T(8,128)(2,1)S(1)} %copy-done.1, bf16[1,1,96,256]{3,2,1,0:T(8,128)(2,1)S(1)} %collective-permute-done, bf16[9,256,256]{2,1,0:T(8,128)(2,1)S(1)} %copy-done.4), kind=kOutput, calls=%fused_computation.94 | convolution fusion | flops 605159424 | bytes 7258112 | tf_op jit(solution)/shard_map/nhwc,cd->nhwd/dot_general | solution.py:35
  41.4 13.0 %fusion.24 = bf16[1,48,96,256]{3,2,1,0:T(8,128)(2,1)S(1)} fusion(f32[48,96,256]{2,1,0:T(8,128)} %fusion.75, f32[48,96,256]{2,1,0:T(8,128)} %fusion.69, f32[48,96,256]{2,1,0:T(8,128)} %fusion.68, f32[48,96,256]{2,1,0:T(8,128)} %fusion.63, f32[48,96,256]{2,1,0:T(8,128)} %fusion.67, f32[48,96,256]{2,1,0:T(8,128)} %fusion.66, f32[48,96,256]{2,1,0:T(8,128)} %fusion.65, ...), kind=kOutput, calls=%fused_computation.33 | convolution fusion | flops 614596608 | bytes 42598400 | tf_op jit(solution)/shard_map/nhwc,cd->nhwd/dot_general | solution.py:35
  54.4 1.4 copy-done.3
  56.5 41.4 %psum.7 = f32[4,256]{1,0:T(4,128)S(1)} all-reduce(f32[4,256]{1,0:T(4,128)S(1)} %pad_maximum_fusion.8), channel_id=1, replica_groups=mesh['rep'=16,'sp'=2] {'rep','sp'}, use_global_device_ids=true, to_apply=%region_4.5 | all-reduce | flops 1024 | bytes 8192 | tf_op jit(solution)/shard_map/psum | solution.py:92
  97.9 0.7 fusion.278
  98.6 0.7 fusion.279
  99.3 1.1 fusion.293
  100.4 5.9 %fusion.292 = (f32[256]{0:T(256)S(1)}, f32[256]{0:T(256)S(1)}, f32[1,48,96,256]{3,2,1,0:T(8,128)}) fusion(f32[256]{0:T(256)S(1)} %get-tuple-element.36, f32[256]{0:T(256)S(1)} %bitcast.465, bf16[1,48,96,256]{3,2,1,0:T(8,128)(2,1)} %copy-done.3, f32[256]{0:T(256)} %bitcast.475, f32[256]{0:T(256)} %bitcast.468, bf16[1,48,96,256]{3,2,1,0:T(8,128)(2,1)} %param.12), kind=kLoop, calls=%fused_computation.319 | loop fusion | flops 20053504 | bytes 9443328 | tf_op jit(solution)/shard_map/reduce_sum | solution.py:182
  106.4 0.7 broadcast_in_dim.8
  107.0 5.1 %all-to-all-start = ((f32[32,4,256]{2,1,0:T(4,128)}), f32[32,4,256]{2,1,0:T(4,128)}, u32[]{:S(2)}, u32[]{:S(2)}) async-start(f32[32,4,256]{2,1,0:T(4,128)} %broadcast_in_dim.8), calls=%async_computation | async-start | bytes 262144 | tf_op jit(solution)/shard_map/all_to_all | solution.py:103
  112.2 8.2 %all-to-all-done = f32[32,4,256]{2,1,0:T(4,128)} async-done(((f32[32,4,256]{2,1,0:T(4,128)}), f32[32,4,256]{2,1,0:T(4,128)}, u32[]{:S(2)}, u32[]{:S(2)}) %all-to-all-start) | async-done | bytes 131104 | tf_op jit(solution)/shard_map/all_to_all | solution.py:103
  120.3 0.9 reduce_sum.113
  121.3 4.4 %fusion.18 = bf16[1,48,96,256]{3,2,1,0:T(8,128)(2,1)S(1)} fusion(bf16[1,48,96,256]{3,2,1,0:T(8,128)(2,1)} %copy-done.3, f32[1,48,96,256]{3,2,1,0:T(8,128)} %get-tuple-element.13, f32[256]{0:T(256)S(1)} %bitcast.471, f32[256]{0:T(256)S(1)} %bitcast.474, f32[256]{0:T(256)S(1)} %get-tuple-element.36, f32[256]{0:T(256)S(1)} %bitcast.466, ...), kind=kLoop, calls=%fused_computation.23 | loop fusion | flops 10616832 | bytes 9442304 | tf_op jit(solution)/shard_map/convert_element_type | solution.py:193
  125.7 0.8 fusion.82
  126.9 0.9 copy-done.5
  127.8 2.9 %fusion.60 = f32[48,96,256]{2,1,0:T(8,128)} fusion(bf16[1,48,96,256]{3,2,1,0:T(8,128)(2,1)S(1)} %fusion.18, bf16[9,256,256]{2,1,0:T(8,128)(2,1)S(1)} %copy-done.5), kind=kOutput, calls=%fused_computation.83 | convolution fusion | flops 603979776 | bytes 7208960 | tf_op jit(solution)/shard_map/nhwd,cd->nhwc/dot_general | solution.py:50
  130.8 2.1 collective-permute-start.6
  132.9 1.3 collective-permute-start.7
  134.2 1.3 collective-permute-start.5
  135.5 3.0 %collective-permute-start.4 = (bf16[1,1,96,256]{3,2,1,0:T(8,128)(2,1)S(1)}, bf16[1,1,96,256]{3,2,1,0:T(8,128)(2,1)S(1)}, u32[]{:S(2)}, u32[]{:S(2)}) collective-permute-start(bf16[1,1,96,256]{3,2,1,0:T(8,128)(2,1)S(1)} %get-tuple-element.16), channel_id=1, source_target_pairs={{0,1},{2,3},{4,5},{6,7},{8,9},{10,11},{12,13},{14,15},{16,17},{18,... | collective-permute-start | bytes 147464 | tf_op jit(solution)/shard_map/ppermute | solution.py:21
  138.5 0.9 fusion.130
  139.5 0.8 fusion.88
  140.3 0.8 fusion.94
  141.1 1.0 fusion.102
  142.2 0.8 fusion.110
  143.0 0.8 fusion.116
  143.8 0.9 fusion.140
  144.8 0.8 fusion.122
  151.0 0.9 fusion.156
  151.9 1.4 select_maximum_fusion
  153.3 3.1 %fusion.31 = f32[48,96,256]{2,1,0:T(8,128)} fusion(bf16[1,50,98,256]{3,2,1,0:T(8,128)(2,1)S(1)} %select_maximum_fusion, bf16[9,256,256]{2,1,0:T(8,128)(2,1)S(1)} %copy-done.5), kind=kOutput, calls=%fused_computation.42 | convolution fusion | flops 603979776 | bytes 7208960 | tf_op jit(solution)/shard_map/nhwd,cd->nhwc/dot_general | solution.py:50
  156.3 2.9 %fusion.32 = f32[48,96,256]{2,1,0:T(8,128)} fusion(bf16[1,50,98,256]{3,2,1,0:T(8,128)(2,1)S(1)} %select_maximum_fusion, bf16[9,256,256]{2,1,0:T(8,128)(2,1)S(1)} %copy-done.5), kind=kOutput, calls=%fused_computation.44 | convolution fusion | flops 603979776 | bytes 7208960 | tf_op jit(solution)/shard_map/nhwd,cd->nhwc/dot_general | solution.py:50
  159.3 3.0 %fusion.33 = f32[48,96,256]{2,1,0:T(8,128)} fusion(bf16[1,50,98,256]{3,2,1,0:T(8,128)(2,1)S(1)} %select_maximum_fusion, bf16[9,256,256]{2,1,0:T(8,128)(2,1)S(1)} %copy-done.5), kind=kOutput, calls=%fused_computation.46 | convolution fusion | flops 603979776 | bytes 7208960 | tf_op jit(solution)/shard_map/nhwd,cd->nhwc/dot_general | solution.py:50
  162.3 1.0 add_convert_fusion.2
  163.3 3.5 %all-to-all-start.1 = ((bf16[4,288,256]{2,1,0:T(8,128)(2,1)}), bf16[4,288,256]{2,1,0:T(8,128)(2,1)S(1)}, u32[]{:S(2)}, u32[]{:S(2)}) async-start(bf16[4,288,256]{2,1,0:T(8,128)(2,1)} %bitcast.116), calls=%async_computation.1 | async-start | bytes 1179648 | tf_op jit(solution)/shard_map/all_to_all | solution.py:86
  166.8 3.9 %fusion.34 = f32[48,96,256]{2,1,0:T(8,128)} fusion(bf16[1,50,98,256]{3,2,1,0:T(8,128)(2,1)S(1)} %select_maximum_fusion, bf16[9,256,256]{2,1,0:T(8,128)(2,1)} %param.9), kind=kOutput, calls=%fused_computation.48 | convolution fusion | flops 603979776 | bytes 7208960 | tf_op jit(solution)/shard_map/nhwd,cd->nhwc/dot_general | solution.py:50
  170.7 3.8 %fusion.39 = f32[48,96,256]{2,1,0:T(8,128)} fusion(bf16[1,50,98,256]{3,2,1,0:T(8,128)(2,1)S(1)} %select_maximum_fusion, bf16[9,256,256]{2,1,0:T(8,128)(2,1)} %param.9), kind=kOutput, calls=%fused_computation.54 | convolution fusion | flops 603979776 | bytes 7208960 | tf_op jit(solution)/shard_map/nhwd,cd->nhwc/dot_general | solution.py:50
  174.6 1.8 all-to-all-done.1
  176.4 0.8 reduce_sum.114
  177.2 3.3 %all-to-all-start.2 = ((bf16[4,72,256]{2,1,0:T(8,128)(2,1)}), bf16[4,72,256]{2,1,0:T(8,128)(2,1)S(1)}, u32[]{:S(2)}, u32[]{:S(2)}) async-start(bf16[4,72,256]{2,1,0:T(8,128)(2,1)} %bitcast.117), calls=%async_computation.2 | async-start | bytes 294912 | tf_op jit(solution)/shard_map/all_to_all | solution.py:86
  180.5 4.6 %fusion.28 = f32[48,96,256]{2,1,0:T(8,128)} fusion(bf16[1,48,96,256]{3,2,1,0:T(8,128)(2,1)} %copy-done, bf16[1,1,96,256]{3,2,1,0:T(8,128)(2,1)S(1)} %collective-permute-done.4, bf16[9,256,256]{2,1,0:T(8,128)(2,1)} %param.9), kind=kOutput, calls=%fused_computation.39 | convolution fusion | flops 605159424 | bytes 7258112 | tf_op jit(solution)/shard_map/nhwd,cd->nhwc/dot_general | solution.py:50
  185.2 1.6 all-to-all-done.2
  187.5 3.4 %all-to-all-start.3 = ((bf16[4,72,256]{2,1,0:T(8,128)(2,1)}), bf16[4,72,256]{2,1,0:T(8,128)(2,1)S(1)}, u32[]{:S(2)}, u32[]{:S(2)}) async-start(bf16[4,72,256]{2,1,0:T(8,128)(2,1)} %broadcast_in_dim.9), calls=%async_computation.3 | async-start | bytes 294912 | tf_op jit(solution)/shard_map/all_to_all | solution.py:86
  190.9 4.7 %fusion.36 = f32[48,96,256]{2,1,0:T(8,128)} fusion(bf16[1,1,96,256]{3,2,1,0:T(8,128)(2,1)S(1)} %collective-permute-done.5, bf16[1,48,96,256]{3,2,1,0:T(8,128)(2,1)} %copy-done, bf16[9,256,256]{2,1,0:T(8,128)(2,1)} %param.9), kind=kOutput, calls=%fused_computation.51 | convolution fusion | flops 605159424 | bytes 7258112 | tf_op jit(solution)/shard_map/nhwd,cd->nhwc/dot_general | solution.py:50
  195.6 1.5 all-to-all-done.3
  197.0 0.9 broadcast_in_dim.11
  197.9 3.5 %all-to-all-start.4 = ((bf16[4,288,256]{2,1,0:T(8,128)(2,1)}), bf16[4,288,256]{2,1,0:T(8,128)(2,1)S(1)}, u32[]{:S(2)}, u32[]{:S(2)}) async-start(bf16[4,288,256]{2,1,0:T(8,128)(2,1)} %broadcast_in_dim.11), calls=%async_computation.4 | async-start | bytes 1179648 | tf_op jit(solution)/shard_map/all_to_all | solution.py:86
  201.4 14.5 %fusion.25 = bf16[1,48,96,256]{3,2,1,0:T(8,128)(2,1)} fusion(f32[48,96,256]{2,1,0:T(8,128)} %fusion.28, f32[48,96,256]{2,1,0:T(8,128)} %fusion.31, f32[48,96,256]{2,1,0:T(8,128)} %fusion.32, f32[48,96,256]{2,1,0:T(8,128)} %fusion.60, f32[48,96,256]{2,1,0:T(8,128)} %fusion.33, f32[48,96,256]{2,1,0:T(8,128)} %fusion.34, f32[48,96,256]{2,1,0:T(8,128)} %fusion.39, ...), kind=kOutput, calls=%fused_computation.34 | convolution fusion | flops 614596608 | bytes 42598400 | tf_op jit(solution)/shard_map/nhwd,cd->nhwc/dot_general | solution.py:50
  215.9 1.1 convert.3
  (88 shorter events, 10.1 us)
Async XLA Ops:
  1.4 15.4 %collective-permute-start.2 = (bf16[1,1,24,256]{3,2,1,0:T(8,128)(2,1)S(1)}, bf16[1,1,24,256]{3,2,1,0:T(8,128)(2,1)S(1)}, u32[]{:S(2)}, u32[]{:S(2)}) collective-permute-start(bf16[1,1,24,256]{3,2,1,0:T(8,128)(2,1)S(1)} %get-tuple-element.21), channel_id=1, source_target_pairs={{0,1},{2,3},{4,5},{6,7},{8,9},{10,11},{12,13},{14,15},{16,17},{18,... | collective-permute-start | bytes 36872 | tf_op jit(solution)/shard_map/ppermute | solution.py:21
  3.7 13.1 %collective-permute-start.3 = (bf16[1,1,24,256]{3,2,1,0:T(8,128)(2,1)S(1)}, bf16[1,1,24,256]{3,2,1,0:T(8,128)(2,1)S(1)}, u32[]{:S(2)}, u32[]{:S(2)}) collective-permute-start(bf16[1,1,24,256]{3,2,1,0:T(8,128)(2,1)S(1)} %get-tuple-element.22), channel_id=1, source_target_pairs={{1,0},{3,2},{5,4},{7,6},{9,8},{11,10},{13,12},{15,14},{17,16},{19,... | collective-permute-start | bytes 36872 | tf_op jit(solution)/shard_map/ppermute | solution.py:23
  5.8 13.6 %collective-permute-start = (bf16[1,1,96,256]{3,2,1,0:T(8,128)(2,1)S(1)}, bf16[1,1,96,256]{3,2,1,0:T(8,128)(2,1)S(1)}, u32[]{:S(2)}, u32[]{:S(2)}) collective-permute-start(bf16[1,1,96,256]{3,2,1,0:T(8,128)(2,1)S(1)} %get-tuple-element.17), channel_id=1, source_target_pairs={{0,1},{2,3},{4,5},{6,7},{8,9},{10,11},{12,13},{14,15},{16,17},{18,... | collective-permute-start | bytes 147464 | tf_op jit(solution)/shard_map/ppermute | solution.py:21
  8.9 10.6 %collective-permute-start.1 = (bf16[1,1,96,256]{3,2,1,0:T(8,128)(2,1)S(1)}, bf16[1,1,96,256]{3,2,1,0:T(8,128)(2,1)S(1)}, u32[]{:S(2)}, u32[]{:S(2)}) collective-permute-start(bf16[1,1,96,256]{3,2,1,0:T(8,128)(2,1)S(1)} %get-tuple-element.18), channel_id=1, source_target_pairs={{1,0},{3,2},{5,4},{7,6},{9,8},{11,10},{13,12},{15,14},{17,16},{19,... | collective-permute-start | bytes 147464 | tf_op jit(solution)/shard_map/ppermute | solution.py:23
  11.5 4.7 %copy-start.17 = (f32[2,256]{1,0:T(2,128)S(1)}, f32[2,256]{1,0:T(2,128)}, u32[]{:S(2)}) copy-start(f32[2,256]{1,0:T(2,128)} %param.11) | copy-start | bytes 6148
  11.5 5.3 %copy-start.6 = (bf16[1,12,24,256]{3,2,1,0:T(8,128)(2,1)S(1)}, bf16[1,12,24,256]{3,2,1,0:T(8,128)(2,1)}, u32[]{:S(2)}) copy-start(bf16[1,12,24,256]{3,2,1,0:T(8,128)(2,1)} %param.8) | copy-start | bytes 442372
  11.5 5.4 %copy-start.4 = (bf16[9,256,256]{2,1,0:T(8,128)(2,1)S(1)}, bf16[9,256,256]{2,1,0:T(8,128)(2,1)}, u32[]{:S(2)}) copy-start(bf16[9,256,256]{2,1,0:T(8,128)(2,1)} %param.9) | copy-start | bytes 3538948
  16.8 1.4 copy-start.13
  16.8 1.8 copy-start.11
  17.7 1.7 copy-start.1
  19.4 19.0 %copy-start.9 = (bf16[1,1,96,256]{3,2,1,0:T(8,128)(2,1)}, bf16[1,1,96,256]{3,2,1,0:T(8,128)(2,1)S(1)}, u32[]{:S(2)}) copy-start(bf16[1,1,96,256]{3,2,1,0:T(8,128)(2,1)S(1)} %collective-permute-done) | copy-start | bytes 147460
  19.4 16.0 %copy-start.7 = (bf16[1,1,96,256]{3,2,1,0:T(8,128)(2,1)}, bf16[1,1,96,256]{3,2,1,0:T(8,128)(2,1)S(1)}, u32[]{:S(2)}) copy-start(bf16[1,1,96,256]{3,2,1,0:T(8,128)(2,1)S(1)} %collective-permute-done.1) | copy-start | bytes 147460
  54.4 1.4 copy-start.3
  55.8 0.7 copy-start.15
  55.8 0.7 copy-start.16
  107.0 13.3 %all-to-all-start = ((f32[32,4,256]{2,1,0:T(4,128)}), f32[32,4,256]{2,1,0:T(4,128)}, u32[]{:S(2)}, u32[]{:S(2)}) async-start(f32[32,4,256]{2,1,0:T(4,128)} %broadcast_in_dim.8), calls=%async_computation | async-start | bytes 262144 | tf_op jit(solution)/shard_map/all_to_all | solution.py:103
  125.7 26.2 %copy-start = (bf16[1,48,96,256]{3,2,1,0:T(8,128)(2,1)}, bf16[1,48,96,256]{3,2,1,0:T(8,128)(2,1)S(1)}, u32[]{:S(2)}) copy-start(bf16[1,48,96,256]{3,2,1,0:T(8,128)(2,1)S(1)} %fusion.18) | copy-start | bytes 7077892
  125.7 2.1 copy-start.5
  127.8 10.7 %copy-start.2 = (bf16[1,48,96,256]{3,2,1,0:T(8,128)(2,1)S(1)}, bf16[1,48,96,256]{3,2,1,0:T(8,128)(2,1)}, u32[]{:S(2)}) copy-start(bf16[1,48,96,256]{3,2,1,0:T(8,128)(2,1)} %param.7) | copy-start | bytes 7077892
  127.8 10.7 %copy-start.10 = (bf16[1,1,96,256]{3,2,1,0:T(8,128)(2,1)S(1)}, bf16[1,1,96,256]{3,2,1,0:T(8,128)(2,1)}, u32[]{:S(2)}) copy-start(bf16[1,1,96,256]{3,2,1,0:T(8,128)(2,1)} %copy-done.9) | copy-start | bytes 147460
  130.8 18.2 %collective-permute-start.6 = (bf16[1,1,24,256]{3,2,1,0:T(8,128)(2,1)S(1)}, bf16[1,1,24,256]{3,2,1,0:T(8,128)(2,1)S(1)}, u32[]{:S(2)}, u32[]{:S(2)}) collective-permute-start(bf16[1,1,24,256]{3,2,1,0:T(8,128)(2,1)S(1)} %get-tuple-element.19), channel_id=1, source_target_pairs={{0,1},{2,3},{4,5},{6,7},{8,9},{10,11},{12,13},{14,15},{16,17},{18,... | collective-permute-start | bytes 36872 | tf_op jit(solution)/shard_map/ppermute | solution.py:21
  132.9 16.1 %collective-permute-start.7 = (bf16[1,1,24,256]{3,2,1,0:T(8,128)(2,1)S(1)}, bf16[1,1,24,256]{3,2,1,0:T(8,128)(2,1)S(1)}, u32[]{:S(2)}, u32[]{:S(2)}) collective-permute-start(bf16[1,1,24,256]{3,2,1,0:T(8,128)(2,1)S(1)} %get-tuple-element.20), channel_id=1, source_target_pairs={{1,0},{3,2},{5,4},{7,6},{9,8},{11,10},{13,12},{15,14},{17,16},{19,... | collective-permute-start | bytes 36872 | tf_op jit(solution)/shard_map/ppermute | solution.py:23
  134.2 17.7 %collective-permute-start.5 = (bf16[1,1,96,256]{3,2,1,0:T(8,128)(2,1)S(1)}, bf16[1,1,96,256]{3,2,1,0:T(8,128)(2,1)S(1)}, u32[]{:S(2)}, u32[]{:S(2)}) collective-permute-start(bf16[1,1,96,256]{3,2,1,0:T(8,128)(2,1)S(1)} %get-tuple-element.15), channel_id=1, source_target_pairs={{1,0},{3,2},{5,4},{7,6},{9,8},{11,10},{13,12},{15,14},{17,16},{19,... | collective-permute-start | bytes 147464 | tf_op jit(solution)/shard_map/ppermute | solution.py:23
  135.5 16.4 %collective-permute-start.4 = (bf16[1,1,96,256]{3,2,1,0:T(8,128)(2,1)S(1)}, bf16[1,1,96,256]{3,2,1,0:T(8,128)(2,1)S(1)}, u32[]{:S(2)}, u32[]{:S(2)}) collective-permute-start(bf16[1,1,96,256]{3,2,1,0:T(8,128)(2,1)S(1)} %get-tuple-element.16), channel_id=1, source_target_pairs={{0,1},{2,3},{4,5},{6,7},{8,9},{10,11},{12,13},{14,15},{16,17},{18,... | collective-permute-start | bytes 147464 | tf_op jit(solution)/shard_map/ppermute | solution.py:21
  143.0 0.8 copy-start.8
  144.8 0.8 copy-start.14
  146.2 1.1 copy-start.12
  148.3 14.0 %collective-permute-start.8 = (bf16[9,128,256]{2,1,0:T(8,128)(2,1)S(1)}, bf16[9,128,256]{2,1,0:T(8,128)(2,1)S(1)}, u32[]{:S(2)}, u32[]{:S(2)}) collective-permute-start(bf16[9,128,256]{2,1,0:T(8,128)(2,1)S(1)} %dynamic-slice_convert_fusion), channel_id=1, source_target_pairs={{0,1},{1,0},{2,3},{3,2},{4,5},{5,4},{6,7},{7,6},{8,9},{9,8},{10,11... | collective-permute-start | bytes 1769480 | tf_op jit(solution)/shard_map/ppermute | solution.py:115
  163.3 13.1 %all-to-all-start.1 = ((bf16[4,288,256]{2,1,0:T(8,128)(2,1)}), bf16[4,288,256]{2,1,0:T(8,128)(2,1)S(1)}, u32[]{:S(2)}, u32[]{:S(2)}) async-start(bf16[4,288,256]{2,1,0:T(8,128)(2,1)} %bitcast.116), calls=%async_computation.1 | async-start | bytes 1179648 | tf_op jit(solution)/shard_map/all_to_all | solution.py:86
  177.2 9.6 %all-to-all-start.2 = ((bf16[4,72,256]{2,1,0:T(8,128)(2,1)}), bf16[4,72,256]{2,1,0:T(8,128)(2,1)S(1)}, u32[]{:S(2)}, u32[]{:S(2)}) async-start(bf16[4,72,256]{2,1,0:T(8,128)(2,1)} %bitcast.117), calls=%async_computation.2 | async-start | bytes 294912 | tf_op jit(solution)/shard_map/all_to_all | solution.py:86
  187.5 9.6 %all-to-all-start.3 = ((bf16[4,72,256]{2,1,0:T(8,128)(2,1)}), bf16[4,72,256]{2,1,0:T(8,128)(2,1)S(1)}, u32[]{:S(2)}, u32[]{:S(2)}) async-start(bf16[4,72,256]{2,1,0:T(8,128)(2,1)} %broadcast_in_dim.9), calls=%async_computation.3 | async-start | bytes 294912 | tf_op jit(solution)/shard_map/all_to_all | solution.py:86
  197.9 18.0 %all-to-all-start.4 = ((bf16[4,288,256]{2,1,0:T(8,128)(2,1)}), bf16[4,288,256]{2,1,0:T(8,128)(2,1)S(1)}, u32[]{:S(2)}, u32[]{:S(2)}) async-start(bf16[4,288,256]{2,1,0:T(8,128)(2,1)} %broadcast_in_dim.11), calls=%async_computation.4 | async-start | bytes 1179648 | tf_op jit(solution)/shard_map/all_to_all | solution.py:86
